TPU v7x, 128 devices: a whole 4x4x4 slice. The times are simulated.
128 devices in a mesh: dp: 64 (over x_hi, z, y, core), feat: 2 (over x_lo).
Axes of the slice: x: 4 (x_hi: 2, x_lo: 2; x = x_hi * 2 + x_lo), y: 4, z: 4, core: 2. Of those that a mesh axis runs over, the one named last changes fastest.
Arguments:
- image_emb: bfloat16 [65536, 1152], P('dp', 'feat'), may hold values from -6 to 6
- text_emb: bfloat16 [65536, 1152], P('dp', 'feat'), may hold values from -6 to 6
- image_ids: int32 [65536], P('dp'), may hold values from 0 to 63
- text_ids: int32 [65536], P('dp'), may hold values from 0 to 63
Outputs:
- row_loss: float32 [65536], P('dp')
- grad_image: float32 [65536, 1152], P('dp', 'feat')
- grad_text: float32 [65536, 1152], P('dp', 'feat')
All inputs are finite; a program needn't handle non-finite values.
Results may differ from a plain program's by a relative error of at most 0.0018.
Values may be sent and summed in bfloat16 or wider, within the bound.
A program may use at most 128 MiB of HBM per device.

v0:
```python
import functools
import math

import jax
import jax.numpy as jnp
from jax import lax
from jax.experimental import pallas as pl
from jax.experimental.pallas import tpu as pltpu
from jax.sharding import PartitionSpec as P

HOPS = 2
MESH = pl.DeviceIdType.MESH
TEMPER = 3.0
BIAS = -4.0

F32 = jnp.float32
BF16 = jnp.bfloat16
LIFT = 2.0**48


def log1p_of(x):
    return jnp.where(x < 1e-3, x * (1.0 - 0.5 * x), jnp.log(1.0 + x))


def join(a, b):
    return a + b + a * b


def code(x):
    x = x * LIFT
    return (x * jnp.abs(x)).astype(BF16)


def decode(y):
    y = y.astype(F32)
    x = jnp.sqrt(jnp.abs(y)) * (1.0 / LIFT)
    return jnp.where(y < 0, -x, x)


def by_rows(n, step, body):
    def at(i, carry):
        body(pl.multiple_of(i * step, step))
        return carry

    lax.fori_loop(0, n // step, at, 0)


def kernel(
    n_dp, n_parts, scale, img, txt, iid, tid, loss_o, gi_o, gt_o,
    X, ST, IDS, SID, GV, GS, CS, CV, YS, YR, XS, RX, LV, LS, LOS, LOR, LFIN,
    xs, xr, cs, cr, ys, yr, ids_s, ids_r, gs_s, gs_r, rs, rr, cvs, cvr, os, orr, los, lor,
):
    WD, R = img.shape
    H = R // 2
    C = R // n_parts
    NH = n_parts // 2
    KW = 2 * WD
    STEP = 96
    d = lax.axis_index("dp")
    f = lax.axis_index("feat")
    n_cell = n_dp // 2
    c = d // 2
    a = lax.rem(d, 2)
    flip = c // (n_cell // 2)
    role = lax.rem(f + flip, 2)
    other = 1 - f
    c_next = lax.rem(c + 1, n_cell)
    c_last = lax.rem(c + n_cell - 1, n_cell)
    f_next = lax.rem(role + c_next // (n_cell // 2), 2)
    f_last = lax.rem(role + c_last // (n_cell // 2), 2)
    partner = (d, other)
    core = (2 * c + 1 - a, f)
    diag = (2 * c + 1 - a, other)

    def nxt(core_index):
        return (2 * c_next + core_index, f_next)

    def last(core_index):
        return (2 * c_last + core_index, f_last)

    own_at = pl.multiple_of(f * WD, WD)
    oth_at = pl.multiple_of(other * WD, WD)
    own_half, oth_half = pl.ds(own_at, WD), pl.ds(oth_at, WD)
    a_part = pl.ds(pl.multiple_of(a * H, H), H)

    def chunk(j):
        return pl.ds(pl.multiple_of(j * C, C), C) if not isinstance(j, int) else pl.ds(j * C, C)

    def rcopy(src, dst, ssem, rsem, dev):
        return pltpu.make_async_remote_copy(
            src_ref=src, dst_ref=dst, send_sem=ssem, recv_sem=rsem, device_id=dev, device_id_type=MESH
        )

    def got(dst, rsem):
        pltpu.make_async_copy(dst, dst, rsem).wait()

    def sent(src, ssem):
        pltpu.make_async_copy(src, src, ssem).wait()

    barrier = pltpu.get_barrier_semaphore()
    peers = [partner, core, diag, nxt(0), nxt(1), last(0), last(1)]
    for dev in peers:
        pl.semaphore_signal(barrier, inc=1, device_id=dev, device_id_type=MESH)
    pl.semaphore_wait(barrier, len(peers))

    raws = (img, txt)

    def send_raw(kind, slot):
        raw = raws[kind]
        for j in range(n_parts):
            rcopy(raw.at[:, chunk(j)], X.at[slot, own_half, chunk(j)], xs.at[kind, j], xr.at[kind, j], partner).start()

    def raw_sent(kind):
        for j in range(n_parts):
            sent(raws[kind].at[:, chunk(j)], xs.at[kind, j])

    def place(kind, slot):
        def some(i):
            X[slot, pl.ds(pl.multiple_of(own_at + i, STEP), STEP), :] = raws[kind][pl.ds(i, STEP), :]

        by_rows(WD, STEP, some)

    def assemble(kind, slot, j):
        got(X.at[slot, oth_half, chunk(j)], xr.at[kind, j])

    def whole(slot, j):
        return X.at[slot, :, chunk(j)]

    def to_core(slot, j):
        rcopy(whole(slot, j), whole(slot, j), cs.at[slot, j], cr.at[slot, j], core).start()

    def from_core(slot, j):
        got(whole(slot, j), cr.at[slot, j])

    def to_core_sent(slot, j):
        sent(whole(slot, j), cs.at[slot, j])

    def move(slot, j, dev):
        rcopy(whole(slot, j), whole(3, j), ys.at[j], yr.at[j], dev).start()

    def ids_to_core(slot):
        rcopy(IDS.at[slot], IDS.at[slot], ids_s.at[slot], ids_r.at[slot], core).start()

    def ids_move(slot, k, dev):
        rcopy(IDS.at[slot], IDS.at[3], ids_s.at[3 + k], ids_r.at[3], dev).start()

    def ids_of(slot):
        got(IDS.at[slot], ids_r.at[slot])

    def column(s_acc, slot):
        for j in range(n_parts):
            row = IDS[slot, 0:1, chunk(j)]
            SID[s_acc, chunk(j), :] = jnp.transpose(jnp.broadcast_to(row, (128, C)))

    def units(pairs, s_slot, s_acc, j, image_rows):
        right = X[s_slot, :, chunk(j)]
        ST[...] = jnp.transpose(right)
        sid = jnp.concatenate([SID[s_acc, chunk(j), :]] * (H // 128), axis=1)
        s_sum = None
        for v, v_slot in pairs:
            left = X[v_slot, :, a_part]
            scores = jnp.dot(ST[...], left, preferred_element_type=F32)
            logits = scale * scores + BIAS
            same = sid == IDS[v_slot, 0:1, a_part]
            z = jnp.where(same, -logits, logits)
            e = jnp.exp(-jnp.abs(z))
            inv = 1.0 / (1.0 + e)
            sig = jnp.where(z >= 0, inv, e * inv)
            w = jnp.where(same, -sig, sig).astype(BF16)
            total, prod = jnp.maximum(z, 0.0), e
            if image_rows:
                while total.shape[0] > 8:
                    n = total.shape[0] // 2
                    total = total[:n] + total[n:]
                    prod = join(prod[:n], prod[n:])
                LV[v] += total + log1p_of(prod)
            else:
                while total.shape[1] > 128:
                    n = total.shape[1] // 2
                    total = total[:, :n] + total[:, n:]
                    prod = join(prod[:, :n], prod[:, n:])
                LS[0, chunk(j), :] += total
                LS[1, chunk(j), :] = join(LS[1, chunk(j), :], prod)
            GV[v] += jnp.dot(right, w, preferred_element_type=F32)
            part = lax.dot_general(left, w, (((1,), (1,)), ((), ())), preferred_element_type=F32)
            s_sum = part if s_sum is None else s_sum + part
        GS[s_acc, :, chunk(j)] = s_sum

    def rows_at(base, i):
        return pl.ds(pl.multiple_of(base + i, STEP), STEP)

    def give(b, k, value, kind, dst, dev):
        def some(i):
            XS[b, pl.ds(i, STEP), chunk(k)] = code(scale * value(rows_at(oth_at, i)))

        by_rows(WD, STEP, some)
        rcopy(XS.at[b, :, chunk(k)], RX.at[kind, :, chunk(dst)], os.at[b, k], orr.at[kind, dst], dev).start()

    def given(b, k):
        sent(XS.at[b, :, chunk(k)], os.at[b, k])

    def keep(out, j, value):
        def some(i):
            out[pl.ds(i, STEP), chunk(j)] = scale * value(rows_at(own_at, i))

        by_rows(WD, STEP, some)

    def keep_taken(out, kind, plus):
        def one(j, carry):
            got(RX.at[kind, :, chunk(j)], orr.at[kind, j])

            def some(i):
                value = decode(RX[kind, pl.ds(i, STEP), chunk(j)])
                out[pl.ds(i, STEP), chunk(j)] = out[pl.ds(i, STEP), chunk(j)] + value if plus else value

            by_rows(WD, STEP, some)
            return carry

        lax.fori_loop(0, n_parts, one, 0)

    def turn_back(v, dev):
        for k in range(NH):

            def some(i):
                YS[pl.ds(i, STEP), chunk(k)] = code(GV[v, pl.ds(i, STEP), chunk(k)])

            by_rows(KW, STEP, some)
            rcopy(YS.at[:, chunk(k)], YR.at[:, chunk(k)], rs.at[k], rr.at[k], dev).start()

    def turned_back():
        for k in range(NH):
            sent(YS.at[:, chunk(k)], rs.at[k])

    def v_value(v, k, returned):
        if returned:
            return lambda rows: GV[v, rows, chunk(k)] + decode(YR[rows, chunk(k)])
        return lambda rows: GV[v, rows, chunk(k)]

    def returned(k):
        got(YR.at[:, chunk(k)], rr.at[k])

    def cv_send(k, value):
        def some(i):
            CV[0, pl.ds(i, STEP), chunk(k)] = scale * value(rows_at(own_at, i))

        by_rows(WD, STEP, some)
        rcopy(CV.at[0, :, chunk(k)], CV.at[1, :, chunk(k)], cvs.at[k], cvr.at[k], core).start()

    def cv_keep(out, k, j):
        got(CV.at[1, :, chunk(k)], cvr.at[k])

        def some(i):
            out[pl.ds(i, STEP), chunk(j)] = CV[1, pl.ds(i, STEP), chunk(k)]

        by_rows(WD, STEP, some)

    def cv_sent():
        for k in range(NH):
            sent(CV.at[0, :, chunk(k)], cvs.at[k])

    def s_part(s_acc, j):
        rcopy(GS.at[s_acc, :, chunk(j)], CS.at[:, chunk(j)], gs_s.at[j], gs_r.at[j], core).start()

    def s_part_sent(s_acc):
        for j in range(n_parts):
            sent(GS.at[s_acc, :, chunk(j)], gs_s.at[j])

    def s_home(s_acc, j, out, b, kind, dev):
        got(CS.at[:, chunk(j)], gs_r.at[j])

        def value(rows):
            return GS[s_acc, rows, chunk(j)] + CS[rows, chunk(j)]

        give(b, j, value, kind, j, dev)
        keep(out, j, value)

    def zero():
        def some(i):
            for v in range(3):
                GV[v, pl.ds(i, STEP), :] = jnp.zeros((STEP, H), F32)

        by_rows(KW, STEP, some)
        LV[...] = jnp.zeros_like(LV)

    def zero_rows():
        def some(i):
            LS[:, pl.ds(i, C), :] = jnp.zeros((2, C, 128), F32)

        by_rows(R, C, some)

    def row_of(v):
        return jnp.broadcast_to(jnp.sum(LV[v], axis=0, keepdims=True), (8, H))

    def row_of_s(start):
        col = LS[0, start : start + H, :] + log1p_of(LS[1, start : start + H, :])
        row = jnp.sum(jnp.transpose(col), axis=0, keepdims=True)
        return jnp.broadcast_to(row, (8, H))

    mean = 1.0 / float((HOPS + 1) * R)

    def loss_out():
        loss_o[...] = LFIN[0:1, :] * mean

    def loss_to_partner():
        rcopy(LFIN, LFIN, los.at[3], lor.at[3], partner).start()

    def role_0():
        @pl.when(a == 0)
        def _():
            send_raw(1, 1)
            IDS[0] = jnp.broadcast_to(iid[...], (8, R))
            IDS[1] = jnp.broadcast_to(tid[...], (8, R))
            ids_to_core(0)
            ids_to_core(1)
            ids_move(0, 0, last(0))
            ids_move(0, 1, last(1))
            place(0, 0)
            place(1, 1)

        @pl.when(a == 1)
        def _():
            send_raw(1, 2)
            send_raw(0, 0)
            IDS[2] = jnp.broadcast_to(tid[...], (8, R))
            ids_to_core(2)
            place(1, 2)

        zero()

        @pl.when(a == 0)
        def _():
            ids_of(2)
            ids_of(3)
            column(0, 2)
            column(1, 1)
            for j in range(n_parts):
                assemble(0, 0, j)
                if j >= NH:
                    to_core(0, j)
                move(0, j, last(j // NH))

        @pl.when(a == 1)
        def _():
            ids_of(0)
            ids_of(1)
            ids_of(3)
            column(0, 2)
            column(1, 1)
            for j in range(n_parts):
                assemble(1, 2, j)
                to_core(2, j)

        for k in range(NH):
            got(whole(3, a * NH + k), yr.at[a * NH + k])

        def first(j, carry):
            pl.when(a == 0)(lambda: from_core(2, j))
            units([(1, 3)], 2, 0, j, True)
            pl.when(a == 0)(lambda: s_part(0, j))

            @pl.when((a == 1) & (j > 0))
            def _():
                s_home(0, j - 1, gt_o, 1, 1, partner)

            return carry

        lax.fori_loop(0, n_parts, first, 0)

        @pl.when(a == 1)
        def _():
            s_home(0, n_parts - 1, gt_o, 1, 1, partner)
            for j in range(NH, n_parts):
                from_core(0, j)

        def second(j, carry):
            @pl.when(a == 0)
            def _():
                assemble(1, 1, j)
                to_core(1, j)

            pl.when(a == 1)(lambda: from_core(1, j))
            units([(0, 0), (1, 3)], 1, 1, j, True)
            pl.when(a == 1)(lambda: s_part(1, j))

            @pl.when((a == 0) & (j > 0))
            def _():
                s_home(1, j - 1, gt_o, 1, 1, partner)

            return carry

        lax.fori_loop(0, n_parts, second, 0)
        turn_back(1, nxt(a))

        LOS[0] = row_of(0)
        LOS[1] = row_of(1)
        rcopy(LOS.at[1], LOR.at[1 + a], los.at[1], lor.at[1 + a], nxt(0)).start()

        @pl.when(a == 1)
        def _():
            rcopy(LOS.at[0], LOR.at[0], los.at[0], lor.at[0], core).start()

        @pl.when(a == 0)
        def _():
            s_home(1, n_parts - 1, gt_o, 1, 1, partner)
            for i in range(3):
                got(LOR.at[i], lor.at[i])
            LFIN[:, 0:H] = LOS[0] + LOR[1]
            LFIN[:, H:R] = LOR[0] + LOR[2]
            loss_to_partner()
            loss_out()
            for k in range(NH):
                returned(k)
                give(0, k, v_value(0, k, True), 0, k, partner)
                keep(gi_o, k, v_value(0, k, True))
            keep_taken(gt_o, 1, True)
            for k in range(NH):
                cv_keep(gi_o, k, NH + k)
            raw_sent(1)
            for j in range(n_parts):
                to_core_sent(1, j)
                sent(whole(0, j), ys.at[j])
            for j in range(NH, n_parts):
                to_core_sent(0, j)
            for k in (0, 1, 3, 4):
                sent(IDS.at[0], ids_s.at[k])
            s_part_sent(0)
            sent(LFIN, los.at[3])

        @pl.when(a == 1)
        def _():
            for k in range(NH):
                returned(k)
                give(0, k, v_value(0, k, True), 0, NH + k, diag)
                cv_send(k, v_value(0, k, True))
            keep_taken(gt_o, 1, True)
            keep_taken(gi_o, 0, False)
            got(LFIN, lor.at[3])
            loss_out()
            raw_sent(0)
            raw_sent(1)
            for j in range(n_parts):
                to_core_sent(2, j)
            sent(IDS.at[2], ids_s.at[2])
            s_part_sent(1)
            sent(LOS.at[0], los.at[0])
            cv_sent()

        for k in range(NH):
            given(0, k)
        for j in range(n_parts):
            given(1, j)
        sent(LOS.at[1], los.at[1])
        turned_back()

    def role_1():
        @pl.when(a == 0)
        def _():
            send_raw(0, 0)
            send_raw(1, 1)
            IDS[1] = jnp.broadcast_to(tid[...], (8, R))
            ids_to_core(1)
            place(1, 1)

        @pl.when(a == 1)
        def _():
            send_raw(1, 2)
            IDS[0] = jnp.broadcast_to(iid[...], (8, R))
            IDS[2] = jnp.broadcast_to(tid[...], (8, R))
            ids_to_core(0)
            ids_to_core(2)
            ids_move(2, 0, nxt(0))
            ids_move(2, 1, nxt(1))
            place(1, 2)
            place(0, 0)

        zero()
        zero_rows()

        @pl.when(a == 0)
        def _():
            ids_of(0)
            ids_of(2)
            ids_of(3)
            column(0, 0)
            for j in range(n_parts):
                assemble(1, 1, j)
                if j >= NH:
                    to_core(1, j)
            for j in range(NH):
                from_core(2, j)

        @pl.when(a == 1)
        def _():
            ids_of(1)
            ids_of(3)
            column(0, 0)
            for j in range(n_parts):
                assemble(1, 2, j)
                if j < NH:
                    to_core(2, j)
                move(2, j, nxt(j // NH))
            for j in range(NH, n_parts):
                from_core(1, j)

        for k in range(NH):
            got(whole(3, a * NH + k), yr.at[a * NH + k])

        def step(j, carry):
            @pl.when(a == 1)
            def _():
                assemble(0, 0, j)
                to_core(0, j)

            pl.when(a == 0)(lambda: from_core(0, j))
            units([(1, 1), (0, 2), (2, 3)], 0, 0, j, False)
            pl.when(a == 0)(lambda: s_part(0, j))

            @pl.when((a == 1) & (j > 0))
            def _():
                s_home(0, j - 1, gi_o, 2, 0, partner)

            return carry

        lax.fori_loop(0, n_parts, step, 0)
        turn_back(2, last(a))

        @pl.when(a == 0)
        def _():
            LOS[0] = row_of_s(0)
            LOS[1] = row_of_s(H)
            for i in range(2):
                rcopy(LOS.at[i], LOR.at[i], los.at[i], lor.at[i], core).start()
            for k in range(NH):
                give(1, k, v_value(1, k, False), 1, k, partner)
                keep(gt_o, k, v_value(1, k, False))
            for k in range(NH):
                returned(k)
                give(0, k, v_value(0, k, True), 1, k, diag)
                cv_send(k, v_value(0, k, True))
            for k in range(NH):
                cv_keep(gt_o, k, NH + k)
            keep_taken(gt_o, 1, True)
            keep_taken(gi_o, 0, False)
            got(LFIN, lor.at[3])
            loss_out()
            raw_sent(0)
            raw_sent(1)
            for j in range(NH, n_parts):
                to_core_sent(1, j)
            sent(IDS.at[1], ids_s.at[1])
            s_part_sent(0)
            for i in range(2):
                sent(LOS.at[i], los.at[i])

        @pl.when(a == 1)
        def _():
            s_home(0, n_parts - 1, gi_o, 2, 0, partner)
            for k in range(NH):
                give(1, k, v_value(1, k, False), 1, NH + k, diag)
                cv_send(k, v_value(1, k, False))
            for i in range(2):
                got(LOR.at[i], lor.at[i])
                LFIN[:, i * H : (i + 1) * H] = row_of_s(i * H) + LOR[i]
            loss_to_partner()
            loss_out()
            for k in range(NH):
                returned(k)
                give(0, k, v_value(0, k, True), 1, NH + k, partner)
                keep(gt_o, NH + k, v_value(0, k, True))
            for k in range(NH):
                cv_keep(gt_o, k, k)
            keep_taken(gt_o, 1, True)
            raw_sent(1)
            for j in range(n_parts):
                to_core_sent(0, j)
                sent(whole(2, j), ys.at[j])
            for j in range(NH):
                to_core_sent(2, j)
            for k in (0, 2, 3, 4):
                sent(IDS.at[0], ids_s.at[k])
            for j in range(n_parts):
                given(2, j)
            sent(LFIN, los.at[3])

        for k in range(NH):
            given(0, k)
            given(1, k)
        turned_back()
        cv_sent()

    pl.when(role == 0)(role_0)
    pl.when(role == 1)(role_1)


def per_device(n_dp, n_parts, image_emb, text_emb, image_ids, text_ids):
    R, width = image_emb.shape
    H, C = R // 2, R // n_parts
    KW = 2 * width
    scale = TEMPER / math.sqrt(KW)
    ids = [i[None, :] for i in (image_ids, text_ids)]
    dma = pltpu.SemaphoreType.DMA
    vmem = pltpu.VMEM
    scratch = [
        vmem((4, KW, R), BF16),
        vmem((C, KW), BF16),
        vmem((4, 8, R), jnp.int32),
        vmem((2, R, 128), jnp.int32),
        vmem((3, KW, H), F32),
        vmem((2, KW, R), F32),
        vmem((KW, R), F32),
        vmem((2, width, H), F32),
        vmem((KW, H), BF16),
        vmem((KW, H), BF16),
        vmem((3, width, R), BF16),
        vmem((2, width, R), BF16),
        vmem((2, 8, H), F32),
        vmem((2, R, 128), F32),
        vmem((2, 8, H), F32),
        vmem((3, 8, H), F32),
        vmem((8, R), F32),
        dma((2, n_parts)), dma((2, n_parts)),
        dma((3, n_parts)), dma((3, n_parts)),
        dma((n_parts,)), dma((n_parts,)),
        dma((5,)), dma((4,)),
        dma((n_parts,)), dma((n_parts,)),
        dma((n_parts,)), dma((n_parts,)),
        dma((n_parts,)), dma((n_parts,)),
        dma((3, n_parts)), dma((2, n_parts)),
        dma((4,)), dma((4,)),
    ]
    flops = 9 * 2 * H * R * KW
    loss, grad_image, grad_text = pl.pallas_call(
        functools.partial(kernel, n_dp, n_parts, scale),
        out_shape=[
            jax.ShapeDtypeStruct((1, R), F32),
            jax.ShapeDtypeStruct((width, R), F32),
            jax.ShapeDtypeStruct((width, R), F32),
        ],
        in_specs=[pl.BlockSpec(memory_space=vmem)] * 4,
        out_specs=[pl.BlockSpec(memory_space=vmem)] * 3,
        scratch_shapes=scratch,
        compiler_params=pltpu.CompilerParams(
            collective_id=0, has_side_effects=True, vmem_limit_bytes=60 * 2**20
        ),
        cost_estimate=pl.CostEstimate(flops=flops, bytes_accessed=12 * R * width, transcendentals=4 * H * R),
    )(image_emb.T, text_emb.T, *ids)
    return (loss[0], grad_image.T, grad_text.T)


def solution(mesh):
    in_specs = (P("dp", "feat"), P("dp", "feat"), P("dp"), P("dp"))
    out_specs = (P("dp"), P("dp", "feat"), P("dp", "feat"))
    body = functools.partial(per_device, mesh.shape["dp"], 4)
    return jax.shard_map(body, mesh=mesh, in_specs=in_specs, out_specs=out_specs, check_vma=False)
```

profile of v0, /device:TPU:2, one launch (start us, length us, event | category | flops | bytes accessed | tf_op | source)
XLA Modules:
  0.0 123.2 jit_solution(6246895215013275504)
XLA Ops:
  0.6 116.4 %shard_map.67 = (f32[1,1024]{1,0:T(1,128)}, f32[576,1024]{1,0:T(8,128)}, f32[576,1024]{1,0:T(8,128)}) custom-call(bf16[576,1024]{1,0:T(8,128)(2,1)} %bitcast.10, bf16[576,1024]{1,0:T(8,128)(2,1)} %bitcast.11, s32[1,1024]{1,0:T(1,128)} %bitcast.12, s32[1,1024]{1,0:T(1,128)} %bitcast.13), custom_call_target="tpu_custom_call" | custom-call | flops 10871635968 | bytes 7077888 | tf_op jit(solution)/shard_map/pallas_call | solution.py:632
  117.0 1.3 %copy.10 = f32[1024]{0:T(1024)} copy(f32[1024]{0:T(1024)} %bitcast.9) | data formatting | bytes 8192
  118.3 0.0 copy-start
  118.3 3.5 %copy.11 = f32[1024,576]{0,1:T(8,128)} copy(f32[1024,576]{0,1:T(8,128)} %bitcast.8) | data formatting | bytes 4718592
  121.8 0.0 copy-done
  121.8 1.4 %copy.12 = f32[1024,576]{0,1:T(8,128)} copy(f32[1024,576]{0,1:T(8,128)S(1)} %bitcast.7) | data formatting | bytes 4718592
Async XLA Ops:
  118.3 3.5 %copy-start = (f32[576,1024]{1,0:T(8,128)S(1)}, f32[576,1024]{1,0:T(8,128)}, u32[]{:S(2)}) copy-start(f32[576,1024]{1,0:T(8,128)} %get-tuple-element.8) | copy-start | bytes 7077892
where the time goes:
time: 123 us
  Pallas kernels  116 us (94%)
  local copies, waits for them, and re-layouts  6.18 us (5%)
    pallas_call x1, Pallas kernels, per_device(): pl.pallas_call(functools.partial(kernel, n_dp, n_parts, scale), out_shape...  116 us
    unnamed x5, local copies, waits for them, and re-layouts  6.18 us

commit v1 on v0

--- a/solution.py
+++ b/solution.py
@@ -16,6 +16,8 @@
 F32 = jnp.float32
 BF16 = jnp.bfloat16
 LIFT = 2.0**48
+LOG2E = 1.4426950408889634
+LN2 = 0.6931471805599453
 
 
 def log1p_of(x):
@@ -54,6 +56,8 @@
     H = R // 2
     C = R // n_parts
     NH = n_parts // 2
+    N_PIECES = R // 128
+    PER = C // 128
     KW = 2 * WD
     STEP = 96
     d = lax.axis_index("dp")
@@ -86,6 +90,9 @@
     def chunk(j):
         return pl.ds(pl.multiple_of(j * C, C), C) if not isinstance(j, int) else pl.ds(j * C, C)
 
+    def piece(q):
+        return pl.ds(pl.multiple_of(q * 128, 128), 128) if not isinstance(q, int) else pl.ds(q * 128, 128)
+
     def rcopy(src, dst, ssem, rsem, dev):
         return pltpu.make_async_remote_copy(
             src_ref=src, dst_ref=dst, send_sem=ssem, recv_sem=rsem, device_id=dev, device_id_type=MESH
@@ -98,10 +105,13 @@
         pltpu.make_async_copy(src, src, ssem).wait()
 
     barrier = pltpu.get_barrier_semaphore()
-    peers = [partner, core, diag, nxt(0), nxt(1), last(0), last(1)]
-    for dev in peers:
-        pl.semaphore_signal(barrier, inc=1, device_id=dev, device_id_type=MESH)
-    pl.semaphore_wait(barrier, len(peers))
+    near = (partner, core, diag)
+
+    def arrive(far, senders):
+        for dev in (*near, far):
+            pl.semaphore_signal(barrier, inc=1, device_id=dev, device_id_type=MESH)
+        pl.when(a == senders)(lambda: pl.semaphore_wait(barrier, len(near) + 2))
+        pl.when(a != senders)(lambda: pl.semaphore_wait(barrier, len(near)))
 
     raws = (img, txt)
 
@@ -152,19 +162,22 @@
             row = IDS[slot, 0:1, chunk(j)]
             SID[s_acc, chunk(j), :] = jnp.transpose(jnp.broadcast_to(row, (128, C)))
 
-    def units(pairs, s_slot, s_acc, j, image_rows):
+    def units(pairs, s_slot, s_acc, j, image_rows, first=True):
         right = X[s_slot, :, chunk(j)]
-        ST[...] = jnp.transpose(right)
+        if first:
+            ST[s_acc, chunk(j), :] = jnp.transpose(right)
         sid = jnp.concatenate([SID[s_acc, chunk(j), :]] * (H // 128), axis=1)
         s_sum = None
-        for v, v_slot in pairs:
-            left = X[v_slot, :, a_part]
-            scores = jnp.dot(ST[...], left, preferred_element_type=F32)
-            logits = scale * scores + BIAS
+        lefts = [X[v_slot, :, a_part] for _, v_slot in pairs]
+        scores = [jnp.dot(ST[s_acc, chunk(j), :], left, preferred_element_type=F32) for left in lefts]
+        for (v, v_slot), left, score in zip(pairs, lefts, scores):
+            logits = (scale * LOG2E) * score + BIAS * LOG2E
             same = sid == IDS[v_slot, 0:1, a_part]
+            e = jnp.exp2(-jnp.abs(logits))
+            den = 1.0 + e
+            inv = pl.reciprocal(den, approx=True)
+            inv = inv * (2.0 - den * inv)
             z = jnp.where(same, -logits, logits)
-            e = jnp.exp(-jnp.abs(z))
-            inv = 1.0 / (1.0 + e)
             sig = jnp.where(z >= 0, inv, e * inv)
             w = jnp.where(same, -sig, sig).astype(BF16)
             total, prod = jnp.maximum(z, 0.0), e
@@ -173,7 +186,7 @@
                     n = total.shape[0] // 2
                     total = total[:n] + total[n:]
                     prod = join(prod[:n], prod[n:])
-                LV[v] += total + log1p_of(prod)
+                LV[v] += LN2 * total + log1p_of(prod)
             else:
                 while total.shape[1] > 128:
                     n = total.shape[1] // 2
@@ -184,79 +197,100 @@
             GV[v] += jnp.dot(right, w, preferred_element_type=F32)
             part = lax.dot_general(left, w, (((1,), (1,)), ((), ())), preferred_element_type=F32)
             s_sum = part if s_sum is None else s_sum + part
-        GS[s_acc, :, chunk(j)] = s_sum
+        if first:
+            GS[s_acc, :, chunk(j)] = s_sum
+        else:
+            GS[s_acc, :, chunk(j)] += s_sum
 
     def rows_at(base, i):
         return pl.ds(pl.multiple_of(base + i, STEP), STEP)
 
-    def give(b, k, value, kind, dst, dev):
+    def give(b, q, value, kind, dst, dev):
         def some(i):
-            XS[b, pl.ds(i, STEP), chunk(k)] = code(scale * value(rows_at(oth_at, i)))
+            XS[b, pl.ds(i, STEP), piece(q)] = code(scale * value(rows_at(oth_at, i)))
 
         by_rows(WD, STEP, some)
-        rcopy(XS.at[b, :, chunk(k)], RX.at[kind, :, chunk(dst)], os.at[b, k], orr.at[kind, dst], dev).start()
-
-    def given(b, k):
-        sent(XS.at[b, :, chunk(k)], os.at[b, k])
-
-    def keep(out, j, value):
+        rcopy(XS.at[b, :, piece(q)], RX.at[kind, :, piece(dst)], os.at[b, q], orr.at[kind, dst], dev).start()
+
+    def given(b, n):
+        def one(q, carry):
+            sent(XS.at[b, :, piece(q)], os.at[b, q])
+            return carry
+
+        lax.fori_loop(0, n, one, 0)
+
+    def keep(out, q, value, plus=False):
         def some(i):
-            out[pl.ds(i, STEP), chunk(j)] = scale * value(rows_at(own_at, i))
+            mine = scale * value(rows_at(own_at, i))
+            out[pl.ds(i, STEP), piece(q)] = out[pl.ds(i, STEP), piece(q)] + mine if plus else mine
 
         by_rows(WD, STEP, some)
 
-    def keep_taken(out, kind, plus):
-        def one(j, carry):
-            got(RX.at[kind, :, chunk(j)], orr.at[kind, j])
-
+    def taken(out, kind, q, plus):
+        got(RX.at[kind, :, piece(q)], orr.at[kind, q])
+
+        def some(i):
+            value = decode(RX[kind, pl.ds(i, STEP), piece(q)])
+            out[pl.ds(i, STEP), piece(q)] = out[pl.ds(i, STEP), piece(q)] + value if plus else value
+
+        by_rows(WD, STEP, some)
+
+    def taken_from_both(out, kind, plus):
+        def one(q):
+            taken(out, kind, q, plus)
+            taken(out, kind, N_PIECES // 2 + q, plus)
+
+        over(N_PIECES // 2, one)
+
+    def over(n, body):
+        def one(q, carry):
+            body(q)
+            return carry
+
+        lax.fori_loop(0, n, one, 0)
+
+    def turn_back(v, dev):
+        def one(q):
             def some(i):
-                value = decode(RX[kind, pl.ds(i, STEP), chunk(j)])
-                out[pl.ds(i, STEP), chunk(j)] = out[pl.ds(i, STEP), chunk(j)] + value if plus else value
+                YS[pl.ds(i, STEP), piece(q)] = code(GV[v, pl.ds(i, STEP), piece(q)])
+
+            by_rows(KW, STEP, some)
+            rcopy(YS.at[:, piece(q)], YR.at[:, piece(q)], rs.at[q], rr.at[q], dev).start()
+
+        over(N_PIECES // 2, one)
+
+    def turned_back():
+        over(N_PIECES // 2, lambda q: sent(YS.at[:, piece(q)], rs.at[q]))
+
+    def v_value(v, q):
+        return lambda rows: GV[v, rows, piece(q)]
+
+    def with_returned(v, q):
+        got(YR.at[:, piece(q)], rr.at[q])
+        return lambda rows: GV[v, rows, piece(q)] + decode(YR[rows, piece(q)])
+
+    def cv_send(q, value):
+        def some(i):
+            CV[0, pl.ds(i, STEP), piece(q)] = scale * value(rows_at(own_at, i))
+
+        by_rows(WD, STEP, some)
+        rcopy(CV.at[0, :, piece(q)], CV.at[1, :, piece(q)], cvs.at[q], cvr.at[q], core).start()
+
+    def cv_keep(out, base, plus=False):
+        def one(q):
+            got(CV.at[1, :, piece(q)], cvr.at[q])
+
+            def some(i):
+                mine = CV[1, pl.ds(i, STEP), piece(q)]
+                at = (pl.ds(i, STEP), piece(base + q))
+                out[at] = out[at] + mine if plus else mine
 
             by_rows(WD, STEP, some)
-            return carry
-
-        lax.fori_loop(0, n_parts, one, 0)
-
-    def turn_back(v, dev):
-        for k in range(NH):
-
-            def some(i):
-                YS[pl.ds(i, STEP), chunk(k)] = code(GV[v, pl.ds(i, STEP), chunk(k)])
-
-            by_rows(KW, STEP, some)
-            rcopy(YS.at[:, chunk(k)], YR.at[:, chunk(k)], rs.at[k], rr.at[k], dev).start()
-
-    def turned_back():
-        for k in range(NH):
-            sent(YS.at[:, chunk(k)], rs.at[k])
-
-    def v_value(v, k, returned):
-        if returned:
-            return lambda rows: GV[v, rows, chunk(k)] + decode(YR[rows, chunk(k)])
-        return lambda rows: GV[v, rows, chunk(k)]
-
-    def returned(k):
-        got(YR.at[:, chunk(k)], rr.at[k])
-
-    def cv_send(k, value):
-        def some(i):
-            CV[0, pl.ds(i, STEP), chunk(k)] = scale * value(rows_at(own_at, i))
-
-        by_rows(WD, STEP, some)
-        rcopy(CV.at[0, :, chunk(k)], CV.at[1, :, chunk(k)], cvs.at[k], cvr.at[k], core).start()
-
-    def cv_keep(out, k, j):
-        got(CV.at[1, :, chunk(k)], cvr.at[k])
-
-        def some(i):
-            out[pl.ds(i, STEP), chunk(j)] = CV[1, pl.ds(i, STEP), chunk(k)]
-
-        by_rows(WD, STEP, some)
+
+        over(N_PIECES // 2, one)
 
     def cv_sent():
-        for k in range(NH):
-            sent(CV.at[0, :, chunk(k)], cvs.at[k])
+        over(N_PIECES // 2, lambda q: sent(CV.at[0, :, piece(q)], cvs.at[q]))
 
     def s_part(s_acc, j):
         rcopy(GS.at[s_acc, :, chunk(j)], CS.at[:, chunk(j)], gs_s.at[j], gs_r.at[j], core).start()
@@ -268,11 +302,16 @@
     def s_home(s_acc, j, out, b, kind, dev):
         got(CS.at[:, chunk(j)], gs_r.at[j])
 
-        def value(rows):
-            return GS[s_acc, rows, chunk(j)] + CS[rows, chunk(j)]
-
-        give(b, j, value, kind, j, dev)
-        keep(out, j, value)
+        def one(i):
+            q = j * PER + i
+
+            def value(rows):
+                return GS[s_acc, rows, piece(q)] + CS[rows, piece(q)]
+
+            give(b, q, value, kind, q, dev)
+            keep(out, q, value)
+
+        over(PER, one)
 
     def zero():
         def some(i):
@@ -292,7 +331,7 @@
         return jnp.broadcast_to(jnp.sum(LV[v], axis=0, keepdims=True), (8, H))
 
     def row_of_s(start):
-        col = LS[0, start : start + H, :] + log1p_of(LS[1, start : start + H, :])
+        col = LN2 * LS[0, start : start + H, :] + log1p_of(LS[1, start : start + H, :])
         row = jnp.sum(jnp.transpose(col), axis=0, keepdims=True)
         return jnp.broadcast_to(row, (8, H))
 
@@ -305,6 +344,8 @@
         rcopy(LFIN, LFIN, los.at[3], lor.at[3], partner).start()
 
     def role_0():
+        arrive(nxt(0), 0)
+
         @pl.when(a == 0)
         def _():
             send_raw(1, 1)
@@ -369,8 +410,6 @@
         @pl.when(a == 1)
         def _():
             s_home(0, n_parts - 1, gt_o, 1, 1, partner)
-            for j in range(NH, n_parts):
-                from_core(0, j)
 
         def second(j, carry):
             @pl.when(a == 0)
@@ -379,7 +418,19 @@
                 to_core(1, j)
 
             pl.when(a == 1)(lambda: from_core(1, j))
-            units([(0, 0), (1, 3)], 1, 1, j, True)
+            units([(1, 3)], 1, 1, j, True)
+            return carry
+
+        lax.fori_loop(0, n_parts, second, 0)
+        turn_back(1, nxt(a))
+
+        @pl.when(a == 1)
+        def _():
+            for j in range(NH, n_parts):
+                from_core(0, j)
+
+        def third(j, carry):
+            units([(0, 0)], 1, 1, j, True, first=False)
             pl.when(a == 1)(lambda: s_part(1, j))
 
             @pl.when((a == 0) & (j > 0))
@@ -388,9 +439,7 @@
 
             return carry
 
-        lax.fori_loop(0, n_parts, second, 0)
-        turn_back(1, nxt(a))
-
+        lax.fori_loop(0, n_parts, third, 0)
         LOS[0] = row_of(0)
         LOS[1] = row_of(1)
         rcopy(LOS.at[1], LOR.at[1 + a], los.at[1], lor.at[1 + a], nxt(0)).start()
@@ -408,13 +457,16 @@
             LFIN[:, H:R] = LOR[0] + LOR[2]
             loss_to_partner()
             loss_out()
-            for k in range(NH):
-                returned(k)
-                give(0, k, v_value(0, k, True), 0, k, partner)
-                keep(gi_o, k, v_value(0, k, True))
-            keep_taken(gt_o, 1, True)
-            for k in range(NH):
-                cv_keep(gi_o, k, NH + k)
+
+            def one(q):
+                value = with_returned(0, q)
+                give(0, q, value, 0, q, partner)
+                keep(gi_o, q, value)
+                taken(gt_o, 1, q, True)
+                taken(gt_o, 1, N_PIECES // 2 + q, True)
+
+            over(N_PIECES // 2, one)
+            cv_keep(gi_o, N_PIECES // 2)
             raw_sent(1)
             for j in range(n_parts):
                 to_core_sent(1, j)
@@ -428,14 +480,17 @@
 
         @pl.when(a == 1)
         def _():
-            for k in range(NH):
-                returned(k)
-                give(0, k, v_value(0, k, True), 0, NH + k, diag)
-                cv_send(k, v_value(0, k, True))
-            keep_taken(gt_o, 1, True)
-            keep_taken(gi_o, 0, False)
+            def one(q):
+                value = with_returned(0, q)
+                give(0, q, value, 0, N_PIECES // 2 + q, diag)
+                cv_send(q, value)
+                taken(gi_o, 0, 2 * q, False)
+                taken(gi_o, 0, 2 * q + 1, False)
+
+            over(N_PIECES // 2, one)
             got(LFIN, lor.at[3])
             loss_out()
+            taken_from_both(gt_o, 1, True)
             raw_sent(0)
             raw_sent(1)
             for j in range(n_parts):
@@ -445,14 +500,14 @@
             sent(LOS.at[0], los.at[0])
             cv_sent()
 
-        for k in range(NH):
-            given(0, k)
-        for j in range(n_parts):
-            given(1, j)
+        given(0, N_PIECES // 2)
+        given(1, N_PIECES)
         sent(LOS.at[1], los.at[1])
         turned_back()
 
     def role_1():
+        arrive(last(1), 1)
+
         @pl.when(a == 0)
         def _():
             send_raw(0, 0)
@@ -512,7 +567,30 @@
                 to_core(0, j)
 
             pl.when(a == 0)(lambda: from_core(0, j))
-            units([(1, 1), (0, 2), (2, 3)], 0, 0, j, False)
+            units([(1, 1), (2, 3)], 0, 0, j, False)
+            return carry
+
+        lax.fori_loop(0, n_parts, step, 0)
+        turn_back(2, last(a))
+
+        @pl.when(a == 0)
+        def _():
+            def own(q):
+                give(1, q, v_value(1, q), 1, q, partner)
+                keep(gt_o, q, v_value(1, q))
+
+            over(N_PIECES // 2, own)
+
+        @pl.when(a == 1)
+        def _():
+            def own(q):
+                give(1, q, v_value(1, q), 1, N_PIECES // 2 + q, diag)
+                cv_send(q, v_value(1, q))
+
+            over(N_PIECES // 2, own)
+
+        def final(j, carry):
+            units([(0, 2)], 0, 0, j, False, first=False)
             pl.when(a == 0)(lambda: s_part(0, j))
 
             @pl.when((a == 1) & (j > 0))
@@ -521,8 +599,7 @@
 
             return carry
 
-        lax.fori_loop(0, n_parts, step, 0)
-        turn_back(2, last(a))
+        lax.fori_loop(0, n_parts, final, 0)
 
         @pl.when(a == 0)
         def _():
@@ -530,19 +607,19 @@
             LOS[1] = row_of_s(H)
             for i in range(2):
                 rcopy(LOS.at[i], LOR.at[i], los.at[i], lor.at[i], core).start()
-            for k in range(NH):
-                give(1, k, v_value(1, k, False), 1, k, partner)
-                keep(gt_o, k, v_value(1, k, False))
-            for k in range(NH):
-                returned(k)
-                give(0, k, v_value(0, k, True), 1, k, diag)
-                cv_send(k, v_value(0, k, True))
-            for k in range(NH):
-                cv_keep(gt_o, k, NH + k)
-            keep_taken(gt_o, 1, True)
-            keep_taken(gi_o, 0, False)
+
+            def one(q):
+                value = with_returned(0, q)
+                give(0, q, value, 1, q, diag)
+                cv_send(q, value)
+                taken(gt_o, 1, 2 * q, True)
+                taken(gt_o, 1, 2 * q + 1, True)
+
+            cv_keep(gt_o, N_PIECES // 2)
+            over(N_PIECES // 2, one)
             got(LFIN, lor.at[3])
             loss_out()
+            taken_from_both(gi_o, 0, False)
             raw_sent(0)
             raw_sent(1)
             for j in range(NH, n_parts):
@@ -555,21 +632,20 @@
         @pl.when(a == 1)
         def _():
             s_home(0, n_parts - 1, gi_o, 2, 0, partner)
-            for k in range(NH):
-                give(1, k, v_value(1, k, False), 1, NH + k, diag)
-                cv_send(k, v_value(1, k, False))
             for i in range(2):
                 got(LOR.at[i], lor.at[i])
                 LFIN[:, i * H : (i + 1) * H] = row_of_s(i * H) + LOR[i]
             loss_to_partner()
             loss_out()
-            for k in range(NH):
-                returned(k)
-                give(0, k, v_value(0, k, True), 1, NH + k, partner)
-                keep(gt_o, NH + k, v_value(0, k, True))
-            for k in range(NH):
-                cv_keep(gt_o, k, k)
-            keep_taken(gt_o, 1, True)
+
+            def one(q):
+                value = with_returned(0, q)
+                give(0, q, value, 1, N_PIECES // 2 + q, partner)
+                keep(gt_o, N_PIECES // 2 + q, value, plus=True)
+
+            over(N_PIECES, lambda q: taken(gt_o, 1, q, False))
+            over(N_PIECES // 2, one)
+            cv_keep(gt_o, 0, plus=True)
             raw_sent(1)
             for j in range(n_parts):
                 to_core_sent(0, j)
@@ -578,13 +654,11 @@
                 to_core_sent(2, j)
             for k in (0, 2, 3, 4):
                 sent(IDS.at[0], ids_s.at[k])
-            for j in range(n_parts):
-                given(2, j)
+            given(2, N_PIECES)
             sent(LFIN, los.at[3])
 
-        for k in range(NH):
-            given(0, k)
-            given(1, k)
+        given(0, N_PIECES // 2)
+        given(1, N_PIECES // 2)
         turned_back()
         cv_sent()
 
@@ -602,7 +676,7 @@
     vmem = pltpu.VMEM
     scratch = [
         vmem((4, KW, R), BF16),
-        vmem((C, KW), BF16),
+        vmem((2, R, KW), BF16),
         vmem((4, 8, R), jnp.int32),
         vmem((2, R, 128), jnp.int32),
         vmem((3, KW, H), F32),
@@ -623,24 +697,24 @@
         dma((n_parts,)), dma((n_parts,)),
         dma((5,)), dma((4,)),
         dma((n_parts,)), dma((n_parts,)),
-        dma((n_parts,)), dma((n_parts,)),
-        dma((n_parts,)), dma((n_parts,)),
-        dma((3, n_parts)), dma((2, n_parts)),
+        dma((R // 256,)), dma((R // 256,)),
+        dma((R // 256,)), dma((R // 256,)),
+        dma((3, R // 128)), dma((2, R // 128)),
         dma((4,)), dma((4,)),
     ]
     flops = 9 * 2 * H * R * KW
     loss, grad_image, grad_text = pl.pallas_call(
         functools.partial(kernel, n_dp, n_parts, scale),
         out_shape=[
-            jax.ShapeDtypeStruct((1, R), F32),
-            jax.ShapeDtypeStruct((width, R), F32),
-            jax.ShapeDtypeStruct((width, R), F32),
+            pltpu.VMEM((1, R), F32),
+            pltpu.VMEM((width, R), F32),
+            pltpu.VMEM((width, R), F32),
         ],
         in_specs=[pl.BlockSpec(memory_space=vmem)] * 4,
         out_specs=[pl.BlockSpec(memory_space=vmem)] * 3,
         scratch_shapes=scratch,
         compiler_params=pltpu.CompilerParams(
-            collective_id=0, has_side_effects=True, vmem_limit_bytes=60 * 2**20
+            collective_id=0, has_side_effects=True, vmem_limit_bytes=54 * 2**20
         ),
         cost_estimate=pl.CostEstimate(flops=flops, bytes_accessed=12 * R * width, transcendentals=4 * H * R),
     )(image_emb.T, text_emb.T, *ids)

time: 123 us -> 103 us (0.84)
  the two profiles are of different devices: /device:TPU:2 before, /device:TPU:1 now
where the time goes in v1:
time: 103 us
  Pallas kernels  98.6 us (96%)
  local copies, waits for them, and re-layouts  3.4 us (3%)
    pallas_call x1, Pallas kernels, per_device(): pl.pallas_call(functools.partial(kernel, n_dp, n_parts, scale), out_shape...  98.6 us
    unnamed x3, local copies, waits for them, and re-layouts  3.4 us

profile of v1, /device:TPU:1, one launch (start us, length us, event | category | flops | bytes accessed | tf_op | source)
XLA Modules:
  0.0 102.6 jit_solution(13432283410629263143)
XLA Ops:
  0.6 98.6 %shard_map.67 = (f32[1,1024]{1,0:T(1,128)S(1)}, f32[576,1024]{1,0:T(8,128)S(1)}, f32[576,1024]{1,0:T(8,128)S(1)}) custom-call(bf16[576,1024]{1,0:T(8,128)(2,1)} %bitcast.10, bf16[576,1024]{1,0:T(8,128)(2,1)} %bitcast.11, s32[1,1024]{1,0:T(1,128)} %bitcast.12, s32[1,1024]{1,0:T(1,128)} %bitcast.13), custom_call_target="tpu_custom_call" | custom-call | flops 10871635968 | bytes 7077888 | tf_op jit(solution)/shard_map/pallas_call | solution.py:706
  99.2 0.6 copy.10
  99.8 1.4 %copy.11 = f32[1024,576]{0,1:T(8,128)} copy(f32[1024,576]{0,1:T(8,128)S(1)} %bitcast.8) | data formatting | bytes 4718592
  101.2 1.4 %copy.12 = f32[1024,576]{0,1:T(8,128)} copy(f32[1024,576]{0,1:T(8,128)S(1)} %bitcast.7) | data formatting | bytes 4718592

commit v2 on v1

--- a/solution.py
+++ b/solution.py
@@ -162,16 +162,28 @@
             row = IDS[slot, 0:1, chunk(j)]
             SID[s_acc, chunk(j), :] = jnp.transpose(jnp.broadcast_to(row, (128, C)))
 
-    def units(pairs, s_slot, s_acc, j, image_rows, first=True):
-        right = X[s_slot, :, chunk(j)]
+    def turned(s_acc, j, image_rows):
+        if image_rows and s_acc == 0:
+            return pl.ds(0, C)
+        return pl.ds(pl.multiple_of(C + j * C, C), C)
+
+    def units(jobs, image_rows, first):
+        rights = [X[s_slot, :, chunk(j)] for _, _, _, s_slot, j in jobs]
+        lefts = [X[v_slot, :, a_part] for _, v_slot, _, _, _ in jobs]
         if first:
-            ST[s_acc, chunk(j), :] = jnp.transpose(right)
-        sid = jnp.concatenate([SID[s_acc, chunk(j), :]] * (H // 128), axis=1)
-        s_sum = None
-        lefts = [X[v_slot, :, a_part] for _, v_slot in pairs]
-        scores = [jnp.dot(ST[s_acc, chunk(j), :], left, preferred_element_type=F32) for left in lefts]
-        for (v, v_slot), left, score in zip(pairs, lefts, scores):
+            done = []
+            for (_, _, s_acc, s_slot, j), right in zip(jobs, rights):
+                if s_slot not in done:
+                    ST[turned(s_acc, j, image_rows), :] = jnp.transpose(right)
+                    done.append(s_slot)
+        scores = [
+            jnp.dot(ST[turned(s_acc, j, image_rows), :], left, preferred_element_type=F32)
+            for (_, _, s_acc, _, j), left in zip(jobs, lefts)
+        ]
+        v_sums, s_sums = {}, {}
+        for (v, v_slot, s_acc, _, j), right, left, score in zip(jobs, rights, lefts, scores):
             logits = (scale * LOG2E) * score + BIAS * LOG2E
+            sid = jnp.concatenate([SID[s_acc, chunk(j), :]] * (H // 128), axis=1)
             same = sid == IDS[v_slot, 0:1, a_part]
             e = jnp.exp2(-jnp.abs(logits))
             den = 1.0 + e
@@ -194,27 +206,35 @@
                     prod = join(prod[:, :n], prod[:, n:])
                 LS[0, chunk(j), :] += total
                 LS[1, chunk(j), :] = join(LS[1, chunk(j), :], prod)
-            GV[v] += jnp.dot(right, w, preferred_element_type=F32)
-            part = lax.dot_general(left, w, (((1,), (1,)), ((), ())), preferred_element_type=F32)
-            s_sum = part if s_sum is None else s_sum + part
-        if first:
-            GS[s_acc, :, chunk(j)] = s_sum
-        else:
-            GS[s_acc, :, chunk(j)] += s_sum
+            v_part = jnp.dot(right, w, preferred_element_type=F32)
+            v_sums[v] = v_sums[v] + v_part if v in v_sums else v_part
+            s_part_of = lax.dot_general(left, w, (((1,), (1,)), ((), ())), preferred_element_type=F32)
+            at = (s_acc, id(j))
+            s_sums[at] = ((s_acc, j), s_sums[at][1] + s_part_of if at in s_sums else s_part_of)
+        for v, value in v_sums.items():
+            GV[v] += value
+        for (s_acc, j), value in s_sums.values():
+            if first:
+                GS[s_acc, :, chunk(j)] = value
+            else:
+                GS[s_acc, :, chunk(j)] += value
 
     def rows_at(base, i):
         return pl.ds(pl.multiple_of(base + i, STEP), STEP)
 
+    def staged(b, q):
+        return piece(b * (N_PIECES // 2) + q)
+
     def give(b, q, value, kind, dst, dev):
         def some(i):
-            XS[b, pl.ds(i, STEP), piece(q)] = code(scale * value(rows_at(oth_at, i)))
+            XS[pl.ds(i, STEP), staged(b, q)] = code(scale * value(rows_at(oth_at, i)))
 
         by_rows(WD, STEP, some)
-        rcopy(XS.at[b, :, piece(q)], RX.at[kind, :, piece(dst)], os.at[b, q], orr.at[kind, dst], dev).start()
+        rcopy(XS.at[:, staged(b, q)], RX.at[kind, :, piece(dst)], os.at[b, q], orr.at[kind, dst], dev).start()
 
     def given(b, n):
         def one(q, carry):
-            sent(XS.at[b, :, piece(q)], os.at[b, q])
+            sent(XS.at[:, staged(b, q)], os.at[b, q])
             return carry
 
         lax.fori_loop(0, n, one, 0)
@@ -391,55 +411,52 @@
                 assemble(1, 2, j)
                 to_core(2, j)
 
+        @pl.when(a == 1)
+        def _():
+            for j in range(NH, n_parts):
+                from_core(0, j)
+
         for k in range(NH):
             got(whole(3, a * NH + k), yr.at[a * NH + k])
 
         def first(j, carry):
-            pl.when(a == 0)(lambda: from_core(2, j))
-            units([(1, 3)], 2, 0, j, True)
-            pl.when(a == 0)(lambda: s_part(0, j))
-
-            @pl.when((a == 1) & (j > 0))
-            def _():
-                s_home(0, j - 1, gt_o, 1, 1, partner)
-
-            return carry
-
-        lax.fori_loop(0, n_parts, first, 0)
-
-        @pl.when(a == 1)
-        def _():
-            s_home(0, n_parts - 1, gt_o, 1, 1, partner)
-
-        def second(j, carry):
             @pl.when(a == 0)
             def _():
                 assemble(1, 1, j)
                 to_core(1, j)
+                from_core(2, j)
 
             pl.when(a == 1)(lambda: from_core(1, j))
-            units([(1, 3)], 1, 1, j, True)
+            units([(1, 3, 0, 2, j), (1, 3, 1, 1, j)], True, True)
+            pl.when(a == 0)(lambda: s_part(0, j))
+
+            @pl.when((a == 1) & (j > 0))
+            def _():
+                s_home(0, j - 1, gt_o, 1, 1, partner)
+
             return carry
 
-        lax.fori_loop(0, n_parts, second, 0)
+        lax.fori_loop(0, n_parts, first, 0)
         turn_back(1, nxt(a))
-
-        @pl.when(a == 1)
-        def _():
-            for j in range(NH, n_parts):
-                from_core(0, j)
-
-        def third(j, carry):
-            units([(0, 0)], 1, 1, j, True, first=False)
-            pl.when(a == 1)(lambda: s_part(1, j))
-
-            @pl.when((a == 0) & (j > 0))
+        pl.when(a == 1)(lambda: s_home(0, n_parts - 1, gt_o, 1, 1, partner))
+
+        def second(i, carry):
+            j = 2 * i
+            units([(0, 0, 1, 1, j), (0, 0, 1, 1, j + 1)], True, False)
+
+            @pl.when(a == 1)
             def _():
+                s_part(1, j)
+                s_part(1, j + 1)
+
+            @pl.when((a == 0) & (i > 0))
+            def _():
+                s_home(1, j - 2, gt_o, 1, 1, partner)
                 s_home(1, j - 1, gt_o, 1, 1, partner)
 
             return carry
 
-        lax.fori_loop(0, n_parts, third, 0)
+        lax.fori_loop(0, NH, second, 0)
         LOS[0] = row_of(0)
         LOS[1] = row_of(1)
         rcopy(LOS.at[1], LOR.at[1 + a], los.at[1], lor.at[1 + a], nxt(0)).start()
@@ -450,6 +467,7 @@
 
         @pl.when(a == 0)
         def _():
+            s_home(1, n_parts - 2, gt_o, 1, 1, partner)
             s_home(1, n_parts - 1, gt_o, 1, 1, partner)
             for i in range(3):
                 got(LOR.at[i], lor.at[i])
@@ -557,9 +575,6 @@
             for j in range(NH, n_parts):
                 from_core(1, j)
 
-        for k in range(NH):
-            got(whole(3, a * NH + k), yr.at[a * NH + k])
-
         def step(j, carry):
             @pl.when(a == 1)
             def _():
@@ -567,11 +582,10 @@
                 to_core(0, j)
 
             pl.when(a == 0)(lambda: from_core(0, j))
-            units([(1, 1), (2, 3)], 0, 0, j, False)
+            units([(0, 2, 0, 0, j), (1, 1, 0, 0, j)], False, True)
             return carry
 
         lax.fori_loop(0, n_parts, step, 0)
-        turn_back(2, last(a))
 
         @pl.when(a == 0)
         def _():
@@ -589,17 +603,27 @@
 
             over(N_PIECES // 2, own)
 
-        def final(j, carry):
-            units([(0, 2)], 0, 0, j, False, first=False)
-            pl.when(a == 0)(lambda: s_part(0, j))
-
-            @pl.when((a == 1) & (j > 0))
+        for k in range(NH):
+            got(whole(3, a * NH + k), yr.at[a * NH + k])
+
+        def final(i, carry):
+            j = 2 * i
+            units([(2, 3, 0, 0, j), (2, 3, 0, 0, j + 1)], False, False)
+
+            @pl.when(a == 0)
             def _():
+                s_part(0, j)
+                s_part(0, j + 1)
+
+            @pl.when((a == 1) & (i > 0))
+            def _():
+                s_home(0, j - 2, gi_o, 2, 0, partner)
                 s_home(0, j - 1, gi_o, 2, 0, partner)
 
             return carry
 
-        lax.fori_loop(0, n_parts, final, 0)
+        lax.fori_loop(0, NH, final, 0)
+        turn_back(2, last(a))
 
         @pl.when(a == 0)
         def _():
@@ -631,6 +655,7 @@
 
         @pl.when(a == 1)
         def _():
+            s_home(0, n_parts - 2, gi_o, 2, 0, partner)
             s_home(0, n_parts - 1, gi_o, 2, 0, partner)
             for i in range(2):
                 got(LOR.at[i], lor.at[i])
@@ -676,7 +701,7 @@
     vmem = pltpu.VMEM
     scratch = [
         vmem((4, KW, R), BF16),
-        vmem((2, R, KW), BF16),
+        vmem((C + R, KW), BF16),
         vmem((4, 8, R), jnp.int32),
         vmem((2, R, 128), jnp.int32),
         vmem((3, KW, H), F32),
@@ -685,7 +710,7 @@
         vmem((2, width, H), F32),
         vmem((KW, H), BF16),
         vmem((KW, H), BF16),
-        vmem((3, width, R), BF16),
+        vmem((width, 2 * R), BF16),
         vmem((2, width, R), BF16),
         vmem((2, 8, H), F32),
         vmem((2, R, 128), F32),
@@ -714,7 +739,7 @@
         out_specs=[pl.BlockSpec(memory_space=vmem)] * 3,
         scratch_shapes=scratch,
         compiler_params=pltpu.CompilerParams(
-            collective_id=0, has_side_effects=True, vmem_limit_bytes=54 * 2**20
+            collective_id=0, has_side_effects=True, vmem_limit_bytes=56 * 2**20
         ),
         cost_estimate=pl.CostEstimate(flops=flops, bytes_accessed=12 * R * width, transcendentals=4 * H * R),
     )(image_emb.T, text_emb.T, *ids)

time: 103 us -> 98 us (0.951)
  Pallas kernels: 98.6 us -> 93.8 us
    pallas_call x1, Pallas kernels: 98.6 us -> 93.8 us  [per_device(): pl.pallas_call(functools.partial(kernel, n_dp, n_parts, scale), out_shape...]
where the time goes in v2:
time: 98 us; the launch traced here: 97.9 us
  Pallas kernels  93.8 us (96%)
  local copies, waits for them, and re-layouts  3.4 us (3%)
    pallas_call x1, Pallas kernels, per_device(): pl.pallas_call(functools.partial(kernel, n_dp, n_parts, scale), out_shape...  93.8 us
    unnamed x3, local copies, waits for them, and re-layouts  3.4 us

profile of v2, /device:TPU:1, one launch (start us, length us, event | category | flops | bytes accessed | tf_op | source)
XLA Modules:
  0.0 97.9 jit_solution(7210066669891050683)
XLA Ops:
  0.6 93.8 %shard_map.67 = (f32[1,1024]{1,0:T(1,128)S(1)}, f32[576,1024]{1,0:T(8,128)S(1)}, f32[576,1024]{1,0:T(8,128)S(1)}) custom-call(bf16[576,1024]{1,0:T(8,128)(2,1)} %bitcast.10, bf16[576,1024]{1,0:T(8,128)(2,1)} %bitcast.11, s32[1,1024]{1,0:T(1,128)} %bitcast.12, s32[1,1024]{1,0:T(1,128)} %bitcast.13), custom_call_target="tpu_custom_call" | custom-call | flops 10871635968 | bytes 7077888 | tf_op jit(solution)/shard_map/pallas_call | solution.py:731
  94.5 0.6 copy.10
  95.0 1.4 %copy.11 = f32[1024,576]{0,1:T(8,128)} copy(f32[1024,576]{0,1:T(8,128)S(1)} %bitcast.8) | data formatting | bytes 4718592
  96.5 1.4 %copy.12 = f32[1024,576]{0,1:T(8,128)} copy(f32[1024,576]{0,1:T(8,128)S(1)} %bitcast.7) | data formatting | bytes 4718592

commit v3 on v2

--- a/solution.py
+++ b/solution.py
@@ -50,7 +50,7 @@
 def kernel(
     n_dp, n_parts, scale, img, txt, iid, tid, loss_o, gi_o, gt_o,
     X, ST, IDS, SID, GV, GS, CS, CV, YS, YR, XS, RX, LV, LS, LOS, LOR, LFIN,
-    xs, xr, cs, cr, ys, yr, ids_s, ids_r, gs_s, gs_r, rs, rr, cvs, cvr, os, orr, los, lor,
+    xs, xr, cs, cr, ys, yr, ids_s, ids_r, gs_s, gs_r, rs, rr, cvs, cvr, os, orr, los, lor, ready,
 ):
     WD, R = img.shape
     H = R // 2
@@ -59,7 +59,7 @@
     N_PIECES = R // 128
     PER = C // 128
     KW = 2 * WD
-    STEP = 96
+    STEP = 576
     d = lax.axis_index("dp")
     f = lax.axis_index("feat")
     n_cell = n_dp // 2
@@ -110,8 +110,16 @@
     def arrive(far, senders):
         for dev in (*near, far):
             pl.semaphore_signal(barrier, inc=1, device_id=dev, device_id_type=MESH)
-        pl.when(a == senders)(lambda: pl.semaphore_wait(barrier, len(near) + 2))
-        pl.when(a != senders)(lambda: pl.semaphore_wait(barrier, len(near)))
+
+        @pl.when(a != senders)
+        def _():
+            pl.semaphore_wait(barrier, len(near))
+            pl.semaphore_signal(ready, inc=1, device_id=partner, device_id_type=MESH)
+
+        pl.when(a == senders)(lambda: pl.semaphore_wait(ready, 1))
+
+    def neighbours_in():
+        pl.semaphore_wait(barrier, len(near) + 2)
 
     raws = (img, txt)
 
@@ -145,8 +153,21 @@
     def to_core_sent(slot, j):
         sent(whole(slot, j), cs.at[slot, j])
 
+    def move_own(kind, j, dev):
+        rcopy(raws[kind].at[:, chunk(j)], X.at[3, own_half, chunk(j)], ys.at[0, j], yr.at[0, j], dev).start()
+
     def move(slot, j, dev):
-        rcopy(whole(slot, j), whole(3, j), ys.at[j], yr.at[j], dev).start()
+        rcopy(X.at[slot, oth_half, chunk(j)], X.at[3, oth_half, chunk(j)], ys.at[1, j], yr.at[1, j], dev).start()
+
+    def move_sent(kind, slot, j):
+        sent(raws[kind].at[:, chunk(j)], ys.at[0, j])
+        sent(X.at[slot, oth_half, chunk(j)], ys.at[1, j])
+
+    def moved_in(f_sender):
+        for k in range(NH):
+            j = a * NH + k
+            for n, half in enumerate((f_sender, 1 - f_sender)):
+                got(X.at[3, pl.ds(pl.multiple_of(half * WD, WD), WD), chunk(j)], yr.at[n, j])
 
     def ids_to_core(slot):
         rcopy(IDS.at[slot], IDS.at[slot], ids_s.at[slot], ids_r.at[slot], core).start()
@@ -369,14 +390,17 @@
         @pl.when(a == 0)
         def _():
             send_raw(1, 1)
+            place(0, 0)
+            place(1, 1)
+            neighbours_in()
             IDS[0] = jnp.broadcast_to(iid[...], (8, R))
             IDS[1] = jnp.broadcast_to(tid[...], (8, R))
             ids_to_core(0)
             ids_to_core(1)
             ids_move(0, 0, last(0))
             ids_move(0, 1, last(1))
-            place(0, 0)
-            place(1, 1)
+            for j in range(n_parts):
+                move_own(0, j, last(j // NH))
 
         @pl.when(a == 1)
         def _():
@@ -416,8 +440,7 @@
             for j in range(NH, n_parts):
                 from_core(0, j)
 
-        for k in range(NH):
-            got(whole(3, a * NH + k), yr.at[a * NH + k])
+        moved_in(f_next)
 
         def first(j, carry):
             @pl.when(a == 0)
@@ -469,26 +492,25 @@
         def _():
             s_home(1, n_parts - 2, gt_o, 1, 1, partner)
             s_home(1, n_parts - 1, gt_o, 1, 1, partner)
+
+            def one(q):
+                value = with_returned(0, q)
+                give(0, q, value, 0, q, partner)
+                keep(gi_o, q, value)
+
+            over(N_PIECES // 2, one)
             for i in range(3):
                 got(LOR.at[i], lor.at[i])
             LFIN[:, 0:H] = LOS[0] + LOR[1]
             LFIN[:, H:R] = LOR[0] + LOR[2]
             loss_to_partner()
             loss_out()
-
-            def one(q):
-                value = with_returned(0, q)
-                give(0, q, value, 0, q, partner)
-                keep(gi_o, q, value)
-                taken(gt_o, 1, q, True)
-                taken(gt_o, 1, N_PIECES // 2 + q, True)
-
-            over(N_PIECES // 2, one)
+            taken_from_both(gt_o, 1, True)
             cv_keep(gi_o, N_PIECES // 2)
             raw_sent(1)
             for j in range(n_parts):
                 to_core_sent(1, j)
-                sent(whole(0, j), ys.at[j])
+                move_sent(0, 0, j)
             for j in range(NH, n_parts):
                 to_core_sent(0, j)
             for k in (0, 1, 3, 4):
@@ -537,14 +559,17 @@
         @pl.when(a == 1)
         def _():
             send_raw(1, 2)
+            place(1, 2)
+            place(0, 0)
+            neighbours_in()
             IDS[0] = jnp.broadcast_to(iid[...], (8, R))
             IDS[2] = jnp.broadcast_to(tid[...], (8, R))
             ids_to_core(0)
             ids_to_core(2)
             ids_move(2, 0, nxt(0))
             ids_move(2, 1, nxt(1))
-            place(1, 2)
-            place(0, 0)
+            for j in range(n_parts):
+                move_own(1, j, nxt(j // NH))
 
         zero()
         zero_rows()
@@ -603,8 +628,7 @@
 
             over(N_PIECES // 2, own)
 
-        for k in range(NH):
-            got(whole(3, a * NH + k), yr.at[a * NH + k])
+        moved_in(f_last)
 
         def final(i, carry):
             j = 2 * i
@@ -674,7 +698,7 @@
             raw_sent(1)
             for j in range(n_parts):
                 to_core_sent(0, j)
-                sent(whole(2, j), ys.at[j])
+                move_sent(1, 2, j)
             for j in range(NH):
                 to_core_sent(2, j)
             for k in (0, 2, 3, 4):
@@ -719,13 +743,14 @@
         vmem((8, R), F32),
         dma((2, n_parts)), dma((2, n_parts)),
         dma((3, n_parts)), dma((3, n_parts)),
-        dma((n_parts,)), dma((n_parts,)),
+        dma((2, n_parts)), dma((2, n_parts)),
         dma((5,)), dma((4,)),
         dma((n_parts,)), dma((n_parts,)),
         dma((R // 256,)), dma((R // 256,)),
         dma((R // 256,)), dma((R // 256,)),
         dma((3, R // 128)), dma((2, R // 128)),
         dma((4,)), dma((4,)),
+        pltpu.SemaphoreType.REGULAR,
     ]
     flops = 9 * 2 * H * R * KW
     loss, grad_image, grad_text = pl.pallas_call(

time: 98 us -> 92.6 us (0.945)
  Pallas kernels: 93.8 us -> 88.4 us
    pallas_call x1, Pallas kernels: 93.8 us -> 88.4 us  [per_device(): pl.pallas_call(functools.partial(kernel, n_dp, n_parts, scale), out_shape...]
where the time goes in v3:
time: 92.6 us; the launch traced here: 92.4 us
  Pallas kernels  88.4 us (95%)
  local copies, waits for them, and re-layouts  3.4 us (4%)
    pallas_call x1, Pallas kernels, per_device(): pl.pallas_call(functools.partial(kernel, n_dp, n_parts, scale), out_shape...  88.4 us
    unnamed x3, local copies, waits for them, and re-layouts  3.4 us

profile of v3, /device:TPU:1, one launch (start us, length us, event | category | flops | bytes accessed | tf_op | source)
XLA Modules:
  0.0 92.4 jit_solution(7526559923991576024)
XLA Ops:
  0.6 88.4 %shard_map.67 = (f32[1,1024]{1,0:T(1,128)S(1)}, f32[576,1024]{1,0:T(8,128)S(1)}, f32[576,1024]{1,0:T(8,128)S(1)}) custom-call(bf16[576,1024]{1,0:T(8,128)(2,1)} %bitcast.10, bf16[576,1024]{1,0:T(8,128)(2,1)} %bitcast.11, s32[1,1024]{1,0:T(1,128)} %bitcast.12, s32[1,1024]{1,0:T(1,128)} %bitcast.13), custom_call_target="tpu_custom_call" | custom-call | flops 10871635968 | bytes 7077888 | tf_op jit(solution)/shard_map/pallas_call | solution.py:756
  89.0 0.6 copy.10
  89.6 1.4 %copy.11 = f32[1024,576]{0,1:T(8,128)} copy(f32[1024,576]{0,1:T(8,128)S(1)} %bitcast.8) | data formatting | bytes 4718592
  91.0 1.4 %copy.12 = f32[1024,576]{0,1:T(8,128)} copy(f32[1024,576]{0,1:T(8,128)S(1)} %bitcast.7) | data formatting | bytes 4718592

commit v4 on v3

--- a/solution.py
+++ b/solution.py
@@ -528,9 +528,9 @@
                 taken(gi_o, 0, 2 * q + 1, False)
 
             over(N_PIECES // 2, one)
+            taken_from_both(gt_o, 1, True)
             got(LFIN, lor.at[3])
             loss_out()
-            taken_from_both(gt_o, 1, True)
             raw_sent(0)
             raw_sent(1)
             for j in range(n_parts):
@@ -614,19 +614,11 @@
 
         @pl.when(a == 0)
         def _():
-            def own(q):
-                give(1, q, v_value(1, q), 1, q, partner)
-                keep(gt_o, q, v_value(1, q))
-
-            over(N_PIECES // 2, own)
-
-        @pl.when(a == 1)
-        def _():
-            def own(q):
-                give(1, q, v_value(1, q), 1, N_PIECES // 2 + q, diag)
-                cv_send(q, v_value(1, q))
-
-            over(N_PIECES // 2, own)
+            over(N_PIECES // 2, lambda q: give(1, q, v_value(1, q), 1, q, partner))
+
+        @pl.when(a == 1)
+        def _():
+            over(N_PIECES // 2, lambda q: give(1, q, v_value(1, q), 1, N_PIECES // 2 + q, diag))
 
         moved_in(f_last)
 
@@ -651,6 +643,7 @@
 
         @pl.when(a == 0)
         def _():
+            over(N_PIECES // 2, lambda q: keep(gt_o, q, v_value(1, q)))
             LOS[0] = row_of_s(0)
             LOS[1] = row_of_s(H)
             for i in range(2):
@@ -665,9 +658,9 @@
 
             cv_keep(gt_o, N_PIECES // 2)
             over(N_PIECES // 2, one)
+            taken_from_both(gi_o, 0, False)
             got(LFIN, lor.at[3])
             loss_out()
-            taken_from_both(gi_o, 0, False)
             raw_sent(0)
             raw_sent(1)
             for j in range(NH, n_parts):
@@ -681,6 +674,7 @@
         def _():
             s_home(0, n_parts - 2, gi_o, 2, 0, partner)
             s_home(0, n_parts - 1, gi_o, 2, 0, partner)
+            over(N_PIECES // 2, lambda q: cv_send(q, v_value(1, q)))
             for i in range(2):
                 got(LOR.at[i], lor.at[i])
                 LFIN[:, i * H : (i + 1) * H] = row_of_s(i * H) + LOR[i]

time: 92.6 us -> 92.6 us (level)
  no operation moved by 1% of the time
where the time goes in v4:
time: 92.6 us; the launch traced here: 92.5 us
  Pallas kernels  88.4 us (95%)
  local copies, waits for them, and re-layouts  3.4 us (4%)
    pallas_call x1, Pallas kernels, per_device(): pl.pallas_call(functools.partial(kernel, n_dp, n_parts, scale), out_shape...  88.4 us
    unnamed x3, local copies, waits for them, and re-layouts  3.4 us

profile of v4, /device:TPU:1, one launch (start us, length us, event | category | flops | bytes accessed | tf_op | source)
XLA Modules:
  0.0 92.5 jit_solution(246686216400039377)
XLA Ops:
  0.6 88.4 %shard_map.67 = (f32[1,1024]{1,0:T(1,128)S(1)}, f32[576,1024]{1,0:T(8,128)S(1)}, f32[576,1024]{1,0:T(8,128)S(1)}) custom-call(bf16[576,1024]{1,0:T(8,128)(2,1)} %bitcast.10, bf16[576,1024]{1,0:T(8,128)(2,1)} %bitcast.11, s32[1,1024]{1,0:T(1,128)} %bitcast.12, s32[1,1024]{1,0:T(1,128)} %bitcast.13), custom_call_target="tpu_custom_call" | custom-call | flops 10871635968 | bytes 7077888 | tf_op jit(solution)/shard_map/pallas_call | solution.py:750
  89.0 0.6 copy.10
  89.6 1.4 %copy.11 = f32[1024,576]{0,1:T(8,128)} copy(f32[1024,576]{0,1:T(8,128)S(1)} %bitcast.8) | data formatting | bytes 4718592
  91.0 1.4 %copy.12 = f32[1024,576]{0,1:T(8,128)} copy(f32[1024,576]{0,1:T(8,128)S(1)} %bitcast.7) | data formatting | bytes 4718592
